TPU v7x, 256 devices: a whole 4x4x8 slice. The times are simulated.
256 devices in a mesh: grp: 8 (over y, core), seq: 32 (over x, z).
Axes of the slice: x: 4, y: 4, z: 8, core: 2. Of those that a mesh axis runs over, the one named last changes fastest.
Arguments:
- video_stream: bfloat16 [8, 32, 256, 1024], P('grp', 'seq'), may hold values from -6 to 6
- video_qkv: bfloat16 [8, 32, 256, 3072], P('grp', 'seq'), may hold values from -6 to 6
- out_weight: bfloat16 [1024, 1024], P(('grp', 'seq')), may hold values from -0.1875 to 0.1875
- text_states: bfloat16 [8, 16384, 3584], P('grp', 'seq'), may hold values from -6 to 6
- query_weight: bfloat16 [3584, 1024], P(('grp', 'seq')), may hold values from -0.09375 to 0.09375
- kv_weight: bfloat16 [1024, 2048], P(('grp', 'seq')), may hold values from -0.1875 to 0.1875
- read_weight: float32 [1024], replicated, may hold values from -0.75 to 0.75
- block_mask: int32 [8, 32, 3], P('grp', 'seq'), may hold values from 0 to 1, as said below
- pair_labels: int32 [8, 32], P('grp', 'seq'), may hold values from 0 to 1
Outputs:
- rewards: float32 [8, 32], P('grp', 'seq')
- loss: float32 [], replicated
- kv_grad: float32 [1024, 2048], P(('grp', 'seq'))
Inputs may be any that keep to these rules, and one draw needn't show every extreme that they name: `block_mask`: column 1 is always 1; column 0 is 0 for segment 0 and column 2 is 0 for segment 32 - 1.
All inputs are finite; a program needn't handle non-finite values.
Results may differ from a plain program's by a relative error of at most 0.0075.
Values may be sent and summed in bfloat16 or wider, within the bound.
A program may use at most 128 MiB of HBM per device.

v0:
```python
import functools
import jax
import jax.numpy as jnp
from jax import lax
from jax.experimental import pallas as pl
from jax.experimental.pallas import tpu as pltpu
from jax.sharding import PartitionSpec as P

HEADS = 16
MESH = pl.DeviceIdType.MESH
EPSILON = 1e-06
NN = (((1,), (0,)), ((), ()))
NT = (((1,), (1,)), ((), ()))
VMEM = pl.BlockSpec(memory_space=pltpu.VMEM)
SMEM = pl.BlockSpec(memory_space=pltpu.SMEM)


def mm(a, b, dims=NN):
    return lax.dot_general(a, b, dims, preferred_element_type=jnp.float32)


def cross_kernel(
    pair_count, mask_ref, label_ref, q_ref, kv, read_ref,
    reward_ref, loss_ref, dkv_ref, vt, exps, inverse, out_t, slopes, d_out_t, d_out,
):
    tokens, width = q_ref.shape
    rows = kv.shape[0] // 3
    pairs = width // 128
    blocks = [pl.ds(b * rows, rows) for b in range(3)]

    lane = lax.broadcasted_iota(jnp.int32, (1, 128), 1)
    sides = [((lane // 64) == h).astype(jnp.bfloat16) for h in range(2)]
    bias = [jnp.where(mask_ref[b] == 1, 0.0, -jnp.inf).astype(jnp.float32) for b in range(3)]

    def forward(j, squares):
        cols = pl.ds(pl.multiple_of(j * 128, 128), 128)
        vcols = pl.ds(pl.multiple_of(width + j * 128, 128), 128)
        vt[cols, :] = kv[:, vcols].T
        k = kv[:, cols]
        q = q_ref[:, cols]
        for h in range(2):
            s = mm(k, q * sides[h], NT)
            s = [s[b * rows : (b + 1) * rows] for b in range(3)]
            top = [jnp.max(s[b], axis=0, keepdims=True) + bias[b] for b in range(3)]
            top = jnp.maximum(jnp.maximum(top[0], top[1]), top[2])
            total = jnp.zeros((1, tokens), jnp.float32)
            for b in range(3):
                e = jnp.exp(s[b] - (top - bias[b]))
                exps[2 * j + h, blocks[b], :] = e
                total = total + jnp.sum(e, axis=0, keepdims=True)
            inv = 1.0 / total
            inverse[2 * j + h] = jnp.broadcast_to(inv, (8, tokens))
            p = (exps[2 * j + h] * inv).astype(jnp.bfloat16)
            mine = pl.ds(pl.multiple_of(j * 128 + h * 64, 64), 64)
            o = mm(vt[mine, :], p)
            out_t[mine, :] = o
            squares = squares + jnp.sum(o * o, axis=0, keepdims=True)
        return squares

    squares = lax.fori_loop(0, pairs, forward, jnp.zeros((1, tokens), jnp.float32))
    inv_root = 1.0 / jnp.sqrt(squares / width + EPSILON)

    def rewards(j, carry):
        reward, inner = carry
        cols = pl.ds(pl.multiple_of(j * 128, 128), 128)
        normed = out_t[cols, :] * inv_root
        gates = jax.nn.sigmoid(normed)
        read = read_ref[cols, 0:1]
        scaled = read * gates
        slope = scaled * (1.0 + normed * (1.0 - gates))
        slopes[cols, :] = slope
        reward = reward + jnp.sum(scaled * normed, axis=0, keepdims=True)
        inner = inner + jnp.sum(slope * normed, axis=0, keepdims=True)
        return reward, inner

    zero = jnp.zeros((1, tokens), jnp.float32)
    reward, inner = lax.fori_loop(0, pairs, rewards, (zero, zero))
    reward = jnp.sum(reward, axis=1, keepdims=True) / tokens
    signed = 2.0 * label_ref[0].astype(jnp.float32) - 1.0
    x = -signed * reward
    loss = jnp.maximum(x, 0.0) + jnp.log1p(jnp.exp(-jnp.abs(x)))
    reward_ref[...] = jnp.broadcast_to(reward, reward_ref.shape)
    loss_ref[...] = jnp.broadcast_to(loss, loss_ref.shape)
    factor = -signed * jax.nn.sigmoid(x) / pair_count / tokens
    inner = inner / width

    @pl.loop(0, pairs)
    def _(j):
        cols = pl.ds(pl.multiple_of(j * 128, 128), 128)
        normed = out_t[cols, :] * inv_root
        d = ((slopes[cols, :] - normed * inner) * (inv_root * factor)).astype(jnp.bfloat16)
        d_out_t[cols, :] = d
        d_out[:, cols] = d.T

    @pl.loop(0, pairs)
    def _(j):
        cols = pl.ds(pl.multiple_of(j * 128, 128), 128)
        vcols = pl.ds(pl.multiple_of(width + j * 128, 128), 128)
        v = kv[:, vcols]
        q = q_ref[:, cols]
        do = d_out[:, cols]
        empty = jnp.zeros((64, tokens), jnp.bfloat16)
        dk = dv = None
        for h in range(2):
            mine = d_out_t[pl.ds(pl.multiple_of(j * 128 + h * 64, 64), 64), :]
            mine = jnp.concatenate([mine, empty] if h == 0 else [empty, mine], axis=0)
            dp = mm(v, mine)
            p = exps[2 * j + h] * inverse[2 * j + h, 0:1, :]
            both = p * dp
            ds = (both - p * jnp.sum(both, axis=0, keepdims=True)).astype(jnp.bfloat16)
            dkh = mm(ds, q * sides[h])
            dvh = mm(p.astype(jnp.bfloat16), do * sides[h])
            dk = dkh if dk is None else dk + dkh
            dv = dvh if dv is None else dv + dvh
        dkv_ref[:, cols] = dk.astype(jnp.bfloat16)
        dkv_ref[:, vcols] = dv.astype(jnp.bfloat16)


def cross(mask, label, q, kv, read, pair_count):
    tokens, width = q.shape
    keys = kv.shape[0]
    f32, bf16 = jnp.float32, jnp.bfloat16
    return pl.pallas_call(
        functools.partial(cross_kernel, pair_count),
        out_shape=(
            jax.ShapeDtypeStruct((8, 128), f32),
            jax.ShapeDtypeStruct((8, 128), f32),
            jax.ShapeDtypeStruct((keys, 2 * width), bf16),
        ),
        in_specs=[SMEM, SMEM] + [VMEM] * 3,
        out_specs=(VMEM, VMEM, VMEM),
        scratch_shapes=[
            pltpu.VMEM((width, keys), bf16),
            pltpu.VMEM((HEADS, keys, tokens), f32),
            pltpu.VMEM((HEADS, 8, tokens), f32),
            pltpu.VMEM((width, tokens), f32),
            pltpu.VMEM((width, tokens), f32),
            pltpu.VMEM((width, tokens), bf16),
            pltpu.VMEM((tokens, width), bf16),
        ],
        compiler_params=pltpu.CompilerParams(vmem_limit_bytes=60 * 2**20),
        name="cross",
    )(mask, label, q, kv, read)


def prepare_kernel(
    qkv_ref, shard_ref, text_ref, stream_ref, q_ref, ctx_ref, kv_ref,
    stage, got, mixed_out, frame, back, text, stream, shards, q_tmp, s_tmp, wq, small, halo,
    local_sem, z_send, z_recv, go_send, go_recv, ret_send, ret_recv, w_send, w_recv, h_send, h_recv,
):
    f32, bf16 = jnp.float32, jnp.bfloat16
    grp, seq = lax.axis_index("grp"), lax.axis_index("seq")
    y, core = grp // 2, grp % 2
    x, z = seq // 8, seq % 8
    width = wq.shape[1]
    rows = frame.shape[0]

    def seq_at(d):
        return ((x + d // 8) % 4) * 8 + (z + d % 8) % 8

    def y_peer(d):
        return (((y + d) % 4) * 2 + core, seq)

    def x_peer(d):
        return (grp, ((x + d) % 4) * 8 + z)

    partner = (y * 2 + 1 - core, seq)
    barrier = pltpu.get_barrier_semaphore()

    locals_ = []
    for part in range(3):
        for side in range(2):
            start = part * width + side * (width // 2)
            locals_.append(pltpu.make_async_copy(
                qkv_ref.at[:, :, start : start + width // 2], stage.at[:, side, part],
                local_sem.at[part * 2 + side],
            ))
    load_text = pltpu.make_async_copy(text_ref, text, local_sem.at[6])
    load_stream = pltpu.make_async_copy(stream_ref, stream, local_sem.at[7])
    for c in locals_ + [load_text, load_stream]:
        c.start()

    @pl.loop(1, 32)
    def _(d):
        pl.semaphore_signal(barrier, inc=1, device_id=(grp, seq_at(d)), device_id_type=MESH)

    for peer in (partner, y_peer(1), y_peer(3)):
        pl.semaphore_signal(barrier, inc=1, device_id=peer, device_id_type=MESH)
    shards[z] = shard_ref[...]
    pl.semaphore_wait(barrier, 34)

    def remote(src, dst, sems, i, peer):
        return pltpu.make_async_remote_copy(
            src_ref=src, dst_ref=dst, send_sem=sems[0].at[i], recv_sem=sems[1].at[i],
            device_id=peer, device_id_type=MESH,
        )

    def z_copy(d):
        return remote(shard_ref, shards.at[z], (z_send, z_recv), d, (grp, x * 8 + (z + d) % 8))

    def go(d):
        t = seq_at(d)
        return remote(stage.at[t // 2, t % 2], got.at[seq], (go_send, go_recv), d, (grp, t))

    def ret(d):
        t = seq_at(d)
        where = (pl.ds(pl.multiple_of(seq // 2 * 16, 16), 16), pl.ds(pl.multiple_of(seq % 2 * (width // 2), 128), width // 2))
        return remote(back.at[t], frame.at[where], (ret_send, ret_recv), d, (grp, t))

    for d in (1, 7, 2, 6, 3, 5, 4):
        z_copy(d).start()
    for c in locals_:
        c.wait()

    @pl.loop(1, 32)
    def _(d):
        go(d).start()

    got[seq] = stage[seq // 2, seq % 2]

    for d in range(1, 8):
        z_copy(d).wait()
    for i in range(8):
        w = shards[i].astype(f32)
        q_tmp[14 * i : 14 * i + 14, :] = w[0:14]
        for k in range(3):
            s_tmp[4 * i : 4 * i + 4, k * width : (k + 1) * width] = w[16 + 4 * k : 20 + 4 * k]

    counter = [0]

    def block(unit, yy, xx, lo, n):
        first = (((y + yy) % 4) * 8 + core * 4 + (x + xx) % 4) * unit + lo
        return pl.ds(pl.multiple_of(first, 16), n)

    def spread(ref, unit, cut, first, second, flip):
        at = (lambda a, b, lo, n: block(unit, b, a, lo, n)) if flip else (lambda a, b, lo, n: block(unit, a, b, lo, n))

        def send(a, b, lo, n, peer):
            i = counter[0]
            counter[0] += 1
            span = at(a, b, lo, n)
            c = remote(ref.at[span, :], ref.at[span, :], (w_send, w_recv), i, peer)
            c.start()
            return c

        started = []

        def out(peer_of, a, b):
            pair = [send(a, b, 0, unit, peer_of(1)), send(a, b, 0, unit, peer_of(3))]
            started.extend(pair)
            return pair

        def on(peer_of, a, b, along_first):
            if along_first:
                pair = [send(a - 1, b, 0, cut, peer_of(1)), send(a + 1, b, cut, unit - cut, peer_of(3))]
            else:
                pair = [send(a, b - 1, 0, cut, peer_of(1)), send(a, b + 1, cut, unit - cut, peer_of(3))]
            started.extend(pair)
            return pair

        def arrived(pair):
            for c in pair:
                c.wait_recv()

        state = {}

        def step0():
            state["f"] = out(first, 0, 0)
            state[0] = out(second, 0, 0)

        def step1():
            arrived(state["f"])
            state["ff"] = on(first, 0, 0, True)
            state[3] = out(second, 3, 0)
            state[1] = out(second, 1, 0)

        def step2():
            arrived(state["ff"])
            state[2] = out(second, 2, 0)

        def forward(a):
            arrived(state[a])
            state["s", a] = on(second, a, 0, False)

        def finish():
            for a in range(4):
                arrived(state["s", a])

        return started, step0, step1, step2, forward, finish

    q_sent, q0, q1, q2, q_on, q_end = spread(wq, 112, 64, x_peer, y_peer, True)
    s_sent, s0, s1, s2, s_on, s_end = spread(small, 32, 16, y_peer, x_peer, False)

    wq[block(112, 0, 0, 0, 112), :] = q_tmp[...].astype(bf16)
    q0()
    small[block(32, 0, 0, 0, 32), :] = s_tmp[...].astype(bf16)
    s0()
    q1()
    s1()
    q2()
    s2()
    for a in (0, 3, 1):
        q_on(a)
        s_on(a)

    @pl.loop(1, 32)
    def _(d):
        go(d).wait_recv()

    count = 32 * 16
    lane = lax.broadcasted_iota(jnp.int32, (1, 128), 1)
    sides = [((lane // 64) == h).astype(bf16) for h in range(2)]

    def temporal(j):
        cols = slice(j * 128, j * 128 + 128)
        q = got[:, 0, :, cols].reshape(count, 128)
        k = got[:, 1, :, cols].reshape(count, 128)
        v = got[:, 2, :, cols].reshape(count, 128)
        other = (
            lax.broadcasted_iota(jnp.int32, (count, count), 0) % 16
            != lax.broadcasted_iota(jnp.int32, (count, count), 1) % 16
        )
        total = None
        for h in range(2):
            s = mm(q * (sides[h] * jnp.asarray(0.125, bf16)), k, NT)
            s = jnp.where(other, -jnp.inf, s)
            e = jnp.exp(s - jnp.max(s, axis=1, keepdims=True))
            p = (e * (1.0 / jnp.sum(e, axis=1, keepdims=True))).astype(bf16)
            o = mm(p, v * sides[h])
            total = o if total is None else total + o
        back[:, :, cols] = total.astype(bf16).reshape(32, 16, 128)

    for j in range(4):
        temporal(j)

    @pl.loop(1, 32)
    def _(d):
        ret(d).start()

    mine = (pl.ds(pl.multiple_of(seq // 2 * 16, 16), 16), pl.ds(pl.multiple_of(seq % 2 * (width // 2), 128), width // 2))
    frame[mine] = back[seq]

    q_on(2)
    s_on(2)

    def to_partner(ref, unit, yy):
        i = counter[0]
        counter[0] += 1
        span = pl.ds(pl.multiple_of((((y + yy) % 4) * 2 + core) * 4 * unit, 16), 4 * unit)
        c = remote(ref.at[span, :], ref.at[span, :], (w_send, w_recv), i, partner)
        c.start()
        return c

    q_core = [to_partner(wq, 112, yy) for yy in (0, 3, 1)]
    s_end()
    s_core = [to_partner(small, 32, yy) for yy in (0, 3, 1, 2)]
    q_end()
    q_core.append(to_partner(wq, 112, 2))

    @pl.loop(1, 32)
    def _(d):
        ret(d).wait_recv()

    for c in s_core:
        c.wait_recv()
    load_stream.wait()

    halos = []
    part = 64
    for i in range(rows // part):
        span = slice(i * part, (i + 1) * part)
        mixed = (stream[span, :].astype(f32) + mm(frame[span, :], small[:, 0:width])).astype(bf16)
        mixed_out[span, :] = mixed
        for s, d in ((0, 1), (1, 31)):
            c = remote(
                mixed_out.at[span, :], halo.at[s, span, :], (h_send, h_recv), 2 * i + s,
                (grp, (seq + d) % 32),
            )
            c.start()
            halos.append(c)

    def keys_values(b, m):
        for c in range(4):
            cols = slice(c * (width // 2), (c + 1) * (width // 2))
            kv_ref[b * rows : (b + 1) * rows, cols] = mm(m, small[:, width + c * (width // 2) : width + (c + 1) * (width // 2)]).astype(bf16)

    ctx_ref[rows : 2 * rows, :] = mixed_out[...]
    keys_values(1, mixed_out[...])
    for c in q_core:
        c.wait_recv()
    load_text.wait()
    tokens = text.shape[0]
    for i in range(2):
        span = slice(i * (tokens // 2), (i + 1) * (tokens // 2))
        for k in range(2):
            cols = slice(k * (width // 2), (k + 1) * (width // 2))
            q_ref[span, cols] = (mm(text[span, :], wq[:, cols]).astype(bf16) * jnp.asarray(0.125, bf16))
    for c in halos:
        c.wait_recv()
    for s, b in ((0, 0), (1, 2)):
        ctx_ref[b * rows : (b + 1) * rows, :] = halo[s]
        keys_values(b, halo[s])

    for c in halos + q_sent + s_sent + q_core + s_core:
        c.wait_send()

    @pl.loop(1, 32)
    def _(d):
        go(d).wait_send()
        ret(d).wait_send()


def prepare(qkv, shard, text, stream):
    f32, bf16 = jnp.float32, jnp.bfloat16
    tokens, depth = text.shape
    rows, width = stream.shape
    any_ = pl.BlockSpec(memory_space=pl.ANY)
    dma = pltpu.SemaphoreType.DMA
    return pl.pallas_call(
        prepare_kernel,
        out_shape=(
            jax.ShapeDtypeStruct((tokens, width), bf16),
            jax.ShapeDtypeStruct((3 * rows, width), bf16),
            jax.ShapeDtypeStruct((3 * rows, 2 * width), bf16),
        ),
        in_specs=[any_, VMEM, any_, any_],
        out_specs=(VMEM, VMEM, VMEM),
        scratch_shapes=[
            pltpu.VMEM((16, 2, 3, 16, width // 2), bf16),
            pltpu.VMEM((32, 3, 16, width // 2), bf16),
            pltpu.VMEM((rows, width), bf16),
            pltpu.VMEM((rows, width), bf16),
            pltpu.VMEM((32, 16, width // 2), bf16),
            pltpu.VMEM((tokens, depth), bf16),
            pltpu.VMEM((rows, width), bf16),
            pltpu.VMEM((8, 32, width), bf16),
            pltpu.VMEM((112, width), f32),
            pltpu.VMEM((32, 3 * width), f32),
            pltpu.VMEM((depth, width), bf16),
            pltpu.VMEM((width, 3 * width), bf16),
            pltpu.VMEM((2, rows, width), bf16),
            dma((8,)), dma((8,)), dma((8,)), dma((32,)), dma((32,)), dma((32,)), dma((32,)),
            dma((64,)), dma((64,)), dma((8,)), dma((8,)),
        ],
        compiler_params=pltpu.CompilerParams(
            collective_id=2, has_side_effects=True, vmem_limit_bytes=56 * 2**20
        ),
        name="prepare",
    )(qkv, shard, text, stream)


def reduce_kernel(
    ctx_ref, dkv_ref, loss_ref, grad_ref, total_ref,
    acc, core_out, core_in, a1_out, a1_in, b1_out, b1_in, a2_out, a2_in, b2_out, b2_in,
    a_sum, b_sum, a3_out, a3_in, b3_out, b3_in, z_out, z_in, l_out, l_in, send, recv,
):
    f32, bf16 = jnp.float32, jnp.bfloat16
    grp, seq = lax.axis_index("grp"), lax.axis_index("seq")
    y, core = grp // 2, grp % 2
    x, z = seq // 8, seq % 8
    rows = ctx_ref.shape[0] // 3
    half = acc.shape[2] // 2
    quarter = half // 2

    def y_peer(d):
        return (((y + d) % 4) * 2 + core, seq)

    def x_peer(d):
        return (grp, ((x + d) % 4) * 8 + z)

    def z_peer(d):
        return (grp, x * 8 + (z + d) % 8)

    partner = (y * 2 + 1 - core, seq)
    peers = [partner] + [y_peer(d) for d in (1, 2, 3)] + [x_peer(d) for d in (1, 2, 3)]
    peers += [z_peer(d) for d in range(1, 8)]
    barrier = pltpu.get_barrier_semaphore()
    for peer in peers:
        pl.semaphore_signal(barrier, inc=1, device_id=peer, device_id_type=MESH)

    count = [0]

    def copy(src, dst, peer):
        i = count[0]
        count[0] += 1
        return pltpu.make_async_remote_copy(
            src_ref=src, dst_ref=dst, send_sem=send.at[i], recv_sem=recv.at[i],
            device_id=peer, device_id_type=MESH,
        )

    def chunk(block, side):
        cols = pl.ds(pl.multiple_of(block * 256 + side * 128, 128), 128)
        parts = [
            mm(ctx_ref[b * rows : (b + 1) * rows, cols].T, dkv_ref[b * rows : (b + 1) * rows, :])
            for b in range(3)
        ]
        return parts[0] + parts[1] + parts[2]

    l_out[0] = loss_ref[...]
    to_core = [copy(core_out.at[i], core_in.at[i], partner) for i in range(4)]
    for i in range(4):
        core_out[i] = chunk((y + 2 + i) % 4, 1 - core).astype(bf16)
        if i == 0:
            pl.semaphore_wait(barrier, len(peers))
            loss_core = copy(l_out.at[0], l_in.at[0], partner)
            loss_core.start()
        to_core[i].start()
    for i in range(4):
        acc[i] = chunk((y + 2 + i) % 4, core)
    loss_core.wait()
    l_out[1] = l_out[0] + l_in[0]
    loss_y = [copy(l_out.at[1], l_in.at[d], y_peer(d)) for d in (1, 2, 3)]
    for c in loss_y:
        c.start()

    to_core[0].wait()
    acc[0] = acc[0] + core_in[0].astype(f32)
    a1 = [copy(a1_out.at[i], a1_in.at[i], y_peer((1, 3)[i])) for i in range(2)]
    for i in range(2):
        a1_out[i] = acc[0, :, i * quarter : (i + 1) * quarter].astype(bf16)
        a1[i].start()
    for i in range(1, 4):
        to_core[i].wait()
        acc[i] = acc[i] + core_in[i].astype(f32)

    def x_rows(d):
        return pl.ds(pl.multiple_of(((x + d) % 4) * 32, 32), 32)

    b1 = [copy(b1_out.at[i], b1_in.at[i], x_peer((1, 3)[i])) for i in range(2)]
    for i in range(2):
        cols = slice(half + i * quarter, half + (i + 1) * quarter)
        b1_out[i] = acc[:, x_rows(2), cols].astype(bf16)
        b1[i].start()

    a2 = [copy(a2_out.at[i], a2_in.at[i], y_peer((1, 3)[i])) for i in range(2)]
    b2 = [copy(b2_out.at[i], b2_in.at[i], x_peer((1, 3)[i])) for i in range(2)]
    for i in range(2):
        lo, hi = slice(i * quarter, (i + 1) * quarter), slice((1 - i) * quarter, (2 - i) * quarter)
        slot = (3, 1)[i]
        a1[i].wait()
        a2_out[i, :, lo] = (acc[slot, :, lo] + a1_in[i].astype(f32)).astype(bf16)
        a2_out[i, :, hi] = acc[slot, :, hi].astype(bf16)
        a2[i].start()
    for i in range(2):
        lo, hi = slice(i * quarter, (i + 1) * quarter), slice((1 - i) * quarter, (2 - i) * quarter)
        mine = slice(half + i * quarter, half + (i + 1) * quarter)
        rest = slice(half + (1 - i) * quarter, half + (2 - i) * quarter)
        d = (1, 3)[i]
        b1[i].wait()
        b2_out[i, :, :, lo] = (acc[:, x_rows(d), mine] + b1_in[i].astype(f32)).astype(bf16)
        b2_out[i, :, :, hi] = acc[:, x_rows(d), rest].astype(bf16)
        b2[i].start()

    for c in loss_y:
        c.wait()
    l_out[2] = l_out[1] + l_in[1] + l_in[2] + l_in[3]
    loss_x = [copy(l_out.at[2], l_in.at[3 + d], x_peer(d)) for d in (1, 2, 3)]
    for c in loss_x:
        c.start()

    a2[0].wait()
    a2[1].wait()
    a_sum[...] = acc[2, :, 0:half] + a2_in[0].astype(f32) + a2_in[1].astype(f32)
    a3 = [copy(a3_out.at[d - 1], a3_in.at[d - 1], x_peer(d)) for d in (1, 2, 3)]
    for d in (1, 2, 3):
        a3_out[d - 1] = a_sum[x_rows(d), :].astype(bf16)
        a3[d - 1].start()
    b2[0].wait()
    b2[1].wait()
    b_sum[...] = acc[:, x_rows(0), half:] + b2_in[0].astype(f32) + b2_in[1].astype(f32)
    b3 = [copy(b3_out.at[d - 1], b3_in.at[d - 1], y_peer(d)) for d in (1, 2, 3)]
    for d in (1, 2, 3):
        b3_out[d - 1] = b_sum[(2 + d) % 4].astype(bf16)
        b3[d - 1].start()

    for c in loss_x:
        c.wait()
    l_out[3] = l_out[2] + l_in[4] + l_in[5] + l_in[6]
    loss_z = [copy(l_out.at[3], l_in.at[6 + d], z_peer(d)) for d in range(1, 8)]
    for c in loss_z:
        c.start()

    for c in a3:
        c.wait()
    a_end = a_sum[x_rows(0), :] + (a3_in[0].astype(f32) + a3_in[1].astype(f32) + a3_in[2].astype(f32))
    for c in b3:
        c.wait()
    b_end = b_sum[2] + (b3_in[0].astype(f32) + b3_in[1].astype(f32) + b3_in[2].astype(f32))
    for i in range(8):
        z_out[i, :, 0:half] = a_end[4 * i : 4 * i + 4]
        z_out[i, :, half:] = b_end[4 * i : 4 * i + 4]
    to_z = [copy(z_out.at[(z + d) % 8], z_in.at[d - 1], z_peer(d)) for d in range(1, 8)]
    for c in to_z:
        c.start()
    for c in loss_z:
        c.wait()
    total = l_out[3]
    for d in range(1, 8):
        total = total + l_in[6 + d]
    total_ref[...] = total
    for c in to_z:
        c.wait()
    grad = z_out[z]
    for d in range(1, 8):
        grad = grad + z_in[d - 1]
    grad_ref[...] = grad


def reduce_grad(ctx, dkv, loss):
    f32, bf16 = jnp.float32, jnp.bfloat16
    width = dkv.shape[1]
    half, quarter = width // 2, width // 4

    def both(*shape):
        return [pltpu.VMEM(shape, bf16), pltpu.VMEM(shape, bf16)]

    return pl.pallas_call(
        reduce_kernel,
        out_shape=(
            jax.ShapeDtypeStruct((4, width), f32),
            jax.ShapeDtypeStruct((8, 128), f32),
        ),
        in_specs=[VMEM] * 3,
        out_specs=(VMEM, VMEM),
        scratch_shapes=[
            pltpu.VMEM((4, 128, width), f32),
            *both(4, 128, width),
            *both(2, 128, quarter),
            *both(2, 4, 32, quarter),
            *both(2, 128, half),
            *both(2, 4, 32, half),
            pltpu.VMEM((128, half), f32),
            pltpu.VMEM((4, 32, half), f32),
            *both(3, 32, half),
            *both(3, 32, half),
            pltpu.VMEM((8, 4, width), f32),
            pltpu.VMEM((7, 4, width), f32),
            pltpu.VMEM((4, 8, 128), f32),
            pltpu.VMEM((14, 8, 128), f32),
            pltpu.SemaphoreType.DMA((39,)),
            pltpu.SemaphoreType.DMA((39,)),
        ],
        compiler_params=pltpu.CompilerParams(
            collective_id=1, has_side_effects=True, vmem_limit_bytes=48 * 2**20
        ),
        name="reduce_grad",
    )(ctx, dkv, loss)


def local(
    video_stream,
    video_qkv,
    out_weight,
    text_states,
    query_weight,
    kv_weight,
    read_weight,
    block_mask,
    pair_labels,
):
    width = out_weight.shape[1]
    rows = video_stream.shape[2]
    shard = jnp.concatenate(
        [
            jnp.pad(query_weight, ((0, 2), (0, 0))),
            out_weight,
            kv_weight[:, :width],
            kv_weight[:, width:],
            jnp.zeros((4, width), jnp.bfloat16),
        ],
        axis=0,
    )
    qkv = video_qkv.reshape(rows // 16, 16, 3 * width)
    queries, context, keys_values = prepare(
        qkv, shard, text_states[0], video_stream.reshape(rows, width)
    )
    pair_count = lax.axis_size("grp") * lax.axis_size("seq")
    read = jnp.broadcast_to(read_weight[:, None], (width, 128))
    reward, loss_value, d_kv = cross(
        block_mask[0, 0], pair_labels[0], queries, keys_values, read, pair_count
    )
    kv_grad, total = reduce_grad(context, d_kv, loss_value)
    return (reward[0:1, 0:1], total[0, 0] / pair_count, kv_grad)


def solution(mesh):
    placed = (
        P("grp", "seq", None, None),
        P("grp", "seq", None, None),
        P(("grp", "seq"), None),
        P("grp", "seq", None),
        P(("grp", "seq"), None),
        P(("grp", "seq"), None),
        P(),
        P("grp", "seq", None),
        P("grp", "seq"),
    )
    return jax.shard_map(
        local,
        mesh=mesh,
        in_specs=placed,
        out_specs=(P("grp", "seq"), P(), P(("grp", "seq"), None)),
        check_vma=False,
    )
```

profile of v0, /device:TPU:2, one launch (start us, length us, event | category | flops | bytes accessed | tf_op | source)
XLA Modules:
  0.0 187.5 jit_solution(5957680402884986390)
XLA Ops:
  1.3 0.7 fusion
  2.0 0.8 pad.4
  2.8 2.5 %concatenate.3.shard_ref = bf16[32,1024]{1,0:T(8,128)(2,1)} concatenate(bf16[16,1024]{1,0:T(8,128)(2,1)S(1)} %pad.4, bf16[4,1024]{1,0:T(4,128)(2,1)} %param.11, bf16[4,1024]{1,0:T(4,128)(2,1)S(1)} %get-tuple-element.20, bf16[4,1024]{1,0:T(4,128)(2,1)S(1)} %get-tuple-element.19, bf16[4,1024]{1,0:T(4,128)(2,1)S(1)} %broadcast_in_dim.4), dimensions={0} | concatenate | bytes 131072 | tf_op jit(solution)/shard_map/concatenate | solution.py:663
  5.3 1.7 broadcast_in_dim.10.read_ref
  7.0 104.8 %prepare.1 = (bf16[512,1024]{1,0:T(8,128)(2,1)}, bf16[768,1024]{1,0:T(8,128)(2,1)}, bf16[768,2048]{1,0:T(8,128)(2,1)}) custom-call(bf16[16,16,3072]{2,1,0:T(8,128)(2,1)} %bitcast.8, bf16[32,1024]{1,0:T(8,128)(2,1)} %concatenate.3.shard_ref, bf16[512,3584]{1,0:T(8,128)(2,1)} %bitcast.7, bf16[256,1024]{1,0:T(8,128)(2,1)} %bitcast.9), custom_call_target="tpu_custom_call" | custom-call | tf_op jit(solution)/shard_map/prepare/pallas_call | solution.py:419
  111.9 0.0 copy-start.1
  111.9 34.4 %cross.1 = (f32[8,128]{1,0:T(8,128)}, f32[8,128]{1,0:T(8,128)}, bf16[768,2048]{1,0:T(8,128)(2,1)}) custom-call(s32[3]{0:T(128)} %bitcast.10, s32[1]{0:T(128)} %bitcast.6.label_ref, bf16[512,1024]{1,0:T(8,128)(2,1)} %get-tuple-element.11.q_ref, bf16[768,2048]{1,0:T(8,128)(2,1)} %get-tuple-element.12.kv, f32[1024,128]{1,0:T(8,128)} %broadcast_in_dim.10.read_ref), custom_call_target="tpu_custom_call" | custom-call | tf_op jit(solution)/shard_map/cross/pallas_call | solution.py:123
  146.2 0.0 copy-done.1
  146.3 0.0 copy-start
  146.3 1.9 %copy-done = bf16[768,2048]{1,0:T(8,128)(2,1)S(1)} copy-done((bf16[768,2048]{1,0:T(8,128)(2,1)S(1)}, bf16[768,2048]{1,0:T(8,128)(2,1)}, u32[]{:S(2)}) %copy-start) | copy-done | bytes 3145752
  148.1 0.0 copy-start.2
  148.1 0.7 copy-done.2
  148.8 34.6 %reduce_grad.1 = (f32[4,2048]{1,0:T(4,128)S(1)}, f32[8,128]{1,0:T(8,128)S(1)}) custom-call(bf16[768,1024]{1,0:T(8,128)(2,1)S(1)} %copy-done.1, bf16[768,2048]{1,0:T(8,128)(2,1)S(1)} %copy-done, f32[8,128]{1,0:T(8,128)S(1)} %copy-done.2), custom_call_target="tpu_custom_call" | custom-call | tf_op jit(solution)/shard_map/reduce_grad/pallas_call | solution.py:617
  183.4 1.2 slice.14
  184.6 0.5 slice.15
  185.8 0.6 copy.14
  (1 shorter events, 0.0 us)
Async XLA Ops:
  111.9 34.4 %copy-start.1 = (bf16[768,1024]{1,0:T(8,128)(2,1)S(1)}, bf16[768,1024]{1,0:T(8,128)(2,1)}, u32[]{:S(2)}) copy-start(bf16[768,1024]{1,0:T(8,128)(2,1)} %get-tuple-element.14.ctx_ref) | copy-start | bytes 4718596
  146.3 1.9 %copy-start = (bf16[768,2048]{1,0:T(8,128)(2,1)S(1)}, bf16[768,2048]{1,0:T(8,128)(2,1)}, u32[]{:S(2)}) copy-start(bf16[768,2048]{1,0:T(8,128)(2,1)} %get-tuple-element.15.dkv_ref) | copy-start | bytes 9437188
  148.1 0.7 copy-start.2
where the time goes:
time: 188 us
  Pallas kernels  174 us (93%)
  local copies, waits for them, and re-layouts  10.7 us (6%)
  between operations  3.09 us (2%)
    pallas_call x1, Pallas kernels, prepare(): pl.pallas_call(prepare_kernel, out_shape=(jax.ShapeDtypeStruct((tokens, w...  105 us
    pallas_call x1, Pallas kernels, reduce_grad(): pl.pallas_call(reduce_kernel, out_shape=(jax.ShapeDtypeStruct((4, width),...  34.6 us
    pallas_call x1, Pallas kernels, cross(): pl.pallas_call(functools.partial(cross_kernel, pair_count), out_shape=(ja...  34.4 us

commit v1 on v0

v1 whole, which is shorter than its diff:
```python
import functools
import jax
import jax.numpy as jnp
from jax import lax
from jax.experimental import pallas as pl
from jax.experimental.pallas import tpu as pltpu
from jax.sharding import PartitionSpec as P

HEADS = 16
MESH = pl.DeviceIdType.MESH
EPSILON = 1e-06
NN = (((1,), (0,)), ((), ()))
NT = (((1,), (1,)), ((), ()))
VMEM = pl.BlockSpec(memory_space=pltpu.VMEM)
SMEM = pl.BlockSpec(memory_space=pltpu.SMEM)


def mm(a, b, dims=NN):
    return lax.dot_general(a, b, dims, preferred_element_type=jnp.float32)


def prepare_kernel(
    qkv_ref, wq_ref, wo_ref, wkv_ref, text_ref, stream_ref, q_ref, ctx_ref, kv_ref,
    shard, stage, got, mixed_out, frame, back, text, stream, shards, q_tmp, s_tmp, wq, small, halo,
    local_sem, z_send, z_recv, go_send, go_recv, ret_send, ret_recv, w_send, w_recv, h_send, h_recv,
):
    f32, bf16 = jnp.float32, jnp.bfloat16
    grp, seq = lax.axis_index("grp"), lax.axis_index("seq")
    y, core = grp // 2, grp % 2
    x, z = seq // 8, seq % 8
    width = wq.shape[1]
    rows = frame.shape[0]

    def seq_at(d):
        return ((x + d // 8) % 4) * 8 + (z + d % 8) % 8

    def y_peer(d):
        return (((y + d) % 4) * 2 + core, seq)

    def x_peer(d):
        return (grp, ((x + d) % 4) * 8 + z)

    partner = (y * 2 + 1 - core, seq)
    barrier = pltpu.get_barrier_semaphore()

    locals_ = []
    for part in range(3):
        for side in range(2):
            start = part * width + side * (width // 2)
            locals_.append(pltpu.make_async_copy(
                qkv_ref.at[:, :, start : start + width // 2], stage.at[:, side, part],
                local_sem.at[part * 2 + side],
            ))
    load_text = pltpu.make_async_copy(text_ref, text, local_sem.at[6])
    load_stream = pltpu.make_async_copy(stream_ref, stream, local_sem.at[7])
    for c in locals_ + [load_text, load_stream]:
        c.start()

    @pl.loop(1, 32)
    def _(d):
        pl.semaphore_signal(barrier, inc=1, device_id=(grp, seq_at(d)), device_id_type=MESH)

    for peer in (partner, y_peer(1), y_peer(3)):
        pl.semaphore_signal(barrier, inc=1, device_id=peer, device_id_type=MESH)
    q_tmp[0:14, :] = wq_ref[...].astype(f32)
    q_tmp[16:20, :] = wo_ref[...].astype(f32)
    q_tmp[20:24, :] = wkv_ref[:, 0:width].astype(f32)
    q_tmp[24:28, :] = wkv_ref[:, width:].astype(f32)
    own = q_tmp[0:32, :].astype(bf16)
    shard[...] = own
    shards[z] = own
    pl.semaphore_wait(barrier, 34)

    def remote(src, dst, sems, i, peer):
        return pltpu.make_async_remote_copy(
            src_ref=src, dst_ref=dst, send_sem=sems[0].at[i], recv_sem=sems[1].at[i],
            device_id=peer, device_id_type=MESH,
        )

    def z_copy(d):
        return remote(shard, shards.at[z], (z_send, z_recv), d, (grp, x * 8 + (z + d) % 8))

    def go(d):
        t = seq_at(d)
        return remote(stage.at[t // 2, t % 2], got.at[seq], (go_send, go_recv), d, (grp, t))

    def ret(d):
        t = seq_at(d)
        where = (pl.ds(pl.multiple_of(seq // 2 * 16, 16), 16), pl.ds(pl.multiple_of(seq % 2 * (width // 2), 128), width // 2))
        return remote(back.at[t], frame.at[where], (ret_send, ret_recv), d, (grp, t))

    for d in (1, 7, 2, 6, 3, 5, 4):
        z_copy(d).start()
    for c in locals_:
        c.wait()

    @pl.loop(1, 32)
    def _(d):
        go(d).start()

    got[seq] = stage[seq // 2, seq % 2]

    for d in range(1, 8):
        z_copy(d).wait()
    for i in range(8):
        w = shards[i].astype(f32)
        q_tmp[14 * i : 14 * i + 14, :] = w[0:14]
        for k in range(3):
            s_tmp[4 * i : 4 * i + 4, k * width : (k + 1) * width] = w[16 + 4 * k : 20 + 4 * k]

    counter = [0]

    def block(unit, yy, xx, lo, n):
        first = (((y + yy) % 4) * 8 + core * 4 + (x + xx) % 4) * unit + lo
        return pl.ds(pl.multiple_of(first, 16), n)

    def spread(ref, unit, cut, first, second, flip):
        at = (lambda a, b, lo, n: block(unit, b, a, lo, n)) if flip else (lambda a, b, lo, n: block(unit, a, b, lo, n))

        def send(a, b, lo, n, peer):
            i = counter[0]
            counter[0] += 1
            span = at(a, b, lo, n)
            c = remote(ref.at[span, :], ref.at[span, :], (w_send, w_recv), i, peer)
            c.start()
            return c

        started = []

        def out(peer_of, a, b):
            pair = [send(a, b, 0, unit, peer_of(1)), send(a, b, 0, unit, peer_of(3))]
            started.extend(pair)
            return pair

        def on(peer_of, a, b, along_first):
            if along_first:
                pair = [send(a - 1, b, 0, cut, peer_of(1)), send(a + 1, b, cut, unit - cut, peer_of(3))]
            else:
                pair = [send(a, b - 1, 0, cut, peer_of(1)), send(a, b + 1, cut, unit - cut, peer_of(3))]
            started.extend(pair)
            return pair

        def arrived(pair):
            for c in pair:
                c.wait_recv()

        state = {}

        def step0():
            state["f"] = out(first, 0, 0)
            state[0] = out(second, 0, 0)

        def step1():
            arrived(state["f"])
            state["ff"] = on(first, 0, 0, True)
            state[3] = out(second, 3, 0)
            state[1] = out(second, 1, 0)

        def step2():
            arrived(state["ff"])
            state[2] = out(second, 2, 0)

        def forward(a):
            arrived(state[a])
            state["s", a] = on(second, a, 0, False)

        def finish():
            for a in range(4):
                arrived(state["s", a])

        return started, step0, step1, step2, forward, finish

    q_sent, q0, q1, q2, q_on, q_end = spread(wq, 112, 64, x_peer, y_peer, True)
    s_sent, s0, s1, s2, s_on, s_end = spread(small, 32, 16, y_peer, x_peer, False)

    wq[block(112, 0, 0, 0, 112), :] = q_tmp[...].astype(bf16)
    q0()
    small[block(32, 0, 0, 0, 32), :] = s_tmp[...].astype(bf16)
    s0()
    q1()
    s1()
    q2()
    s2()
    for a in (0, 3, 1):
        q_on(a)
        s_on(a)

    @pl.loop(1, 32)
    def _(d):
        go(d).wait_recv()

    count = 32 * 16
    lane = lax.broadcasted_iota(jnp.int32, (1, 128), 1)
    sides = [((lane // 64) == h).astype(bf16) for h in range(2)]

    def temporal(j):
        cols = slice(j * 128, j * 128 + 128)
        q = got[:, 0, :, cols].reshape(count, 128)
        k = got[:, 1, :, cols].reshape(count, 128)
        v = got[:, 2, :, cols].reshape(count, 128)
        other = (
            lax.broadcasted_iota(jnp.int32, (count, count), 0) % 16
            != lax.broadcasted_iota(jnp.int32, (count, count), 1) % 16
        )
        total = None
        for h in range(2):
            s = mm(q * (sides[h] * jnp.asarray(0.125, bf16)), k, NT)
            s = jnp.where(other, -jnp.inf, s)
            e = jnp.exp(s - jnp.max(s, axis=1, keepdims=True))
            p = (e * (1.0 / jnp.sum(e, axis=1, keepdims=True))).astype(bf16)
            o = mm(p, v * sides[h])
            total = o if total is None else total + o
        back[:, :, cols] = total.astype(bf16).reshape(32, 16, 128)

    for j in range(4):
        temporal(j)

    @pl.loop(1, 32)
    def _(d):
        ret(d).start()

    mine = (pl.ds(pl.multiple_of(seq // 2 * 16, 16), 16), pl.ds(pl.multiple_of(seq % 2 * (width // 2), 128), width // 2))
    frame[mine] = back[seq]

    q_on(2)
    s_on(2)

    def to_partner(ref, unit, yy):
        i = counter[0]
        counter[0] += 1
        span = pl.ds(pl.multiple_of((((y + yy) % 4) * 2 + core) * 4 * unit, 16), 4 * unit)
        c = remote(ref.at[span, :], ref.at[span, :], (w_send, w_recv), i, partner)
        c.start()
        return c

    q_core = [to_partner(wq, 112, yy) for yy in (0, 3, 1)]
    s_end()
    s_core = [to_partner(small, 32, yy) for yy in (0, 3, 1, 2)]
    q_end()
    q_core.append(to_partner(wq, 112, 2))

    @pl.loop(1, 32)
    def _(d):
        ret(d).wait_recv()

    for c in s_core:
        c.wait_recv()
    load_stream.wait()

    halos = []
    part = 64
    for i in range(rows // part):
        span = slice(i * part, (i + 1) * part)
        mixed = (stream[span, :].astype(f32) + mm(frame[span, :], small[:, 0:width])).astype(bf16)
        mixed_out[span, :] = mixed
        for s, d in ((0, 1), (1, 31)):
            c = remote(
                mixed_out.at[span, :], halo.at[s, span, :], (h_send, h_recv), 2 * i + s,
                (grp, (seq + d) % 32),
            )
            c.start()
            halos.append(c)

    def keys_values(b, m):
        for c in range(4):
            cols = slice(c * (width // 2), (c + 1) * (width // 2))
            kv_ref[b * rows : (b + 1) * rows, cols] = mm(m, small[:, width + c * (width // 2) : width + (c + 1) * (width // 2)]).astype(bf16)

    ctx_ref[rows : 2 * rows, :] = mixed_out[...]
    keys_values(1, mixed_out[...])
    for c in q_core:
        c.wait_recv()
    load_text.wait()
    tokens = text.shape[0]
    for i in range(2):
        span = slice(i * (tokens // 2), (i + 1) * (tokens // 2))
        for k in range(2):
            cols = slice(k * (width // 2), (k + 1) * (width // 2))
            q_ref[span, cols] = (mm(text[span, :], wq[:, cols]).astype(bf16) * jnp.asarray(0.125, bf16))
    for c in halos:
        c.wait_recv()
    for s, b in ((0, 0), (1, 2)):
        ctx_ref[b * rows : (b + 1) * rows, :] = halo[s]
        keys_values(b, halo[s])

    for c in halos + q_sent + s_sent + q_core + s_core:
        c.wait_send()

    @pl.loop(1, 32)
    def _(d):
        go(d).wait_send()
        ret(d).wait_send()


def prepare(qkv, wq, wo, wkv, text, stream):
    f32, bf16 = jnp.float32, jnp.bfloat16
    tokens, depth = text.shape
    rows, width = stream.shape
    any_ = pl.BlockSpec(memory_space=pl.ANY)
    dma = pltpu.SemaphoreType.DMA
    return pl.pallas_call(
        prepare_kernel,
        out_shape=(
            jax.ShapeDtypeStruct((tokens, width), bf16),
            jax.ShapeDtypeStruct((3 * rows, width), bf16),
            jax.ShapeDtypeStruct((3 * rows, 2 * width), bf16),
        ),
        in_specs=[any_, VMEM, VMEM, VMEM, any_, any_],
        out_specs=(VMEM, VMEM, VMEM),
        scratch_shapes=[
            pltpu.VMEM((32, width), bf16),
            pltpu.VMEM((16, 2, 3, 16, width // 2), bf16),
            pltpu.VMEM((32, 3, 16, width // 2), bf16),
            pltpu.VMEM((rows, width), bf16),
            pltpu.VMEM((rows, width), bf16),
            pltpu.VMEM((32, 16, width // 2), bf16),
            pltpu.VMEM((tokens, depth), bf16),
            pltpu.VMEM((rows, width), bf16),
            pltpu.VMEM((8, 32, width), bf16),
            pltpu.VMEM((112, width), f32),
            pltpu.VMEM((32, 3 * width), f32),
            pltpu.VMEM((depth, width), bf16),
            pltpu.VMEM((width, 3 * width), bf16),
            pltpu.VMEM((2, rows, width), bf16),
            dma((8,)), dma((8,)), dma((8,)), dma((32,)), dma((32,)), dma((32,)), dma((32,)),
            dma((64,)), dma((64,)), dma((8,)), dma((8,)),
        ],
        compiler_params=pltpu.CompilerParams(
            collective_id=2, has_side_effects=True, vmem_limit_bytes=56 * 2**20
        ),
        name="prepare",
    )(qkv, wq, wo, wkv, text, stream)


def reward_kernel(
    pair_count, mask_ref, label_ref, q_ref, kv, read_ref, ctx_ref, reward_ref, total_ref, grad_ref,
    vt, exps, inverse, d_out_t, d_out, ctx_t, dkv,
    acc, core_out, core_in, a1_out, a1_in, b1_out, b1_in, a2_out, a2_in, b2_out, b2_in,
    a_sum, b_sum, a3_out, a3_in, b3_out, b3_in, z_out, z_in, l_out, l_in, send, recv,
):
    f32, bf16 = jnp.float32, jnp.bfloat16
    tokens, width = q_ref.shape
    rows = kv.shape[0] // 3
    pairs = width // 128
    blocks = [pl.ds(b * rows, rows) for b in range(3)]
    grp, seq = lax.axis_index("grp"), lax.axis_index("seq")
    y, core = grp // 2, grp % 2
    x, z = seq // 8, seq % 8
    half = width // 2
    quarter = half // 2

    def y_peer(d):
        return (((y + d) % 4) * 2 + core, seq)

    def x_peer(d):
        return (grp, ((x + d) % 4) * 8 + z)

    def z_peer(d):
        return (grp, x * 8 + (z + d) % 8)

    partner = (y * 2 + 1 - core, seq)
    peers = [partner] + [y_peer(d) for d in (1, 2, 3)] + [x_peer(d) for d in (1, 2, 3)]
    peers += [z_peer(d) for d in range(1, 8)]
    barrier = pltpu.get_barrier_semaphore()
    for peer in peers:
        pl.semaphore_signal(barrier, inc=1, device_id=peer, device_id_type=MESH)

    count = [0]

    def copy(src, dst, peer):
        i = count[0]
        count[0] += 1
        c = pltpu.make_async_remote_copy(
            src_ref=src, dst_ref=dst, send_sem=send.at[i], recv_sem=recv.at[i],
            device_id=peer, device_id_type=MESH,
        )
        c.start()
        return c

    lane = lax.broadcasted_iota(jnp.int32, (1, 128), 1)
    sides = [((lane // 64) == h).astype(bf16) for h in range(2)]
    bias = [jnp.where(mask_ref[b] == 1, 0.0, -jnp.inf).astype(f32) for b in range(3)]

    def forward(j, squares):
        cols = pl.ds(pl.multiple_of(j * 128, 128), 128)
        vcols = pl.ds(pl.multiple_of(width + j * 128, 128), 128)
        vt[cols, :] = kv[:, vcols].T
        ctx_t[cols, :] = ctx_ref[:, cols].T
        k = kv[:, cols]
        q = q_ref[:, cols]
        for h in range(2):
            s = mm(k, q * sides[h], NT)
            s = [s[b * rows : (b + 1) * rows] for b in range(3)]
            top = [jnp.max(s[b], axis=0, keepdims=True) + bias[b] for b in range(3)]
            top = jnp.maximum(jnp.maximum(top[0], top[1]), top[2])
            total = jnp.zeros((1, tokens), f32)
            for b in range(3):
                e = jnp.exp(s[b] - (top - bias[b]))
                exps[2 * j + h, blocks[b], :] = e
                total = total + jnp.sum(e, axis=0, keepdims=True)
            inv = 1.0 / total
            inverse[2 * j + h] = jnp.broadcast_to(inv, (8, tokens))
            p = (exps[2 * j + h] * inv).astype(bf16)
            mine = pl.ds(pl.multiple_of(j * 128 + h * 64, 64), 64)
            o = mm(vt[mine, :], p)
            acc[j // 4, j % 4, h * 64 : h * 64 + 64, tokens:] = o
            squares = squares + jnp.sum(o * o, axis=0, keepdims=True)
        return squares

    squares = lax.fori_loop(0, pairs, forward, jnp.zeros((1, tokens), f32))
    inv_root = 1.0 / jnp.sqrt(squares / width + EPSILON)

    reward = jnp.zeros((1, tokens), f32)
    inner = jnp.zeros((1, tokens), f32)
    for j in range(pairs):
        normed = acc[j // 4, j % 4, :, tokens:] * inv_root
        gates = jax.nn.sigmoid(normed)
        read = jnp.broadcast_to(read_ref[j : j + 1, :], (128, 128)).T[:, 0:1]
        scaled = read * gates
        slope = scaled * (1.0 + normed * (1.0 - gates))
        acc[j // 4, j % 4, :, 0:tokens] = slope
        reward = reward + jnp.sum(scaled * normed, axis=0, keepdims=True)
        inner = inner + jnp.sum(slope * normed, axis=0, keepdims=True)

    reward = jnp.sum(reward, axis=1, keepdims=True) / tokens
    signed = 2.0 * label_ref[0].astype(f32) - 1.0
    margin = -signed * reward
    loss = jnp.maximum(margin, 0.0) + jnp.log1p(jnp.exp(-jnp.abs(margin)))
    reward_ref[...] = reward
    l_out[0] = jnp.broadcast_to(loss, (8, 128))
    pl.semaphore_wait(barrier, len(peers))
    loss_core = copy(l_out.at[0], l_in.at[0], partner)
    factor = -signed * jax.nn.sigmoid(margin) / pair_count / tokens
    inner = inner / width

    @pl.loop(0, pairs)
    def _(j):
        cols = pl.ds(pl.multiple_of(j * 128, 128), 128)
        normed = acc[j // 4, j % 4, :, tokens:] * inv_root
        d = ((acc[j // 4, j % 4, :, 0:tokens] - normed * inner) * (inv_root * factor)).astype(bf16)
        d_out_t[cols, :] = d
        d_out[:, cols] = d.T

    def backward(j):
        cols = pl.ds(pl.multiple_of(j * 128, 128), 128)
        vcols = pl.ds(pl.multiple_of(width + j * 128, 128), 128)
        v = kv[:, vcols]
        q = q_ref[:, cols]
        do = d_out[:, cols]
        empty = jnp.zeros((64, tokens), bf16)
        dk = dv = None
        for h in range(2):
            mine = d_out_t[pl.ds(pl.multiple_of(j * 128 + h * 64, 64), 64), :]
            mine = jnp.concatenate([mine, empty] if h == 0 else [empty, mine], axis=0)
            dp = mm(v, mine)
            p = exps[2 * j + h] * inverse[2 * j + h, 0:1, :]
            both = p * dp
            ds = (both - p * jnp.sum(both, axis=0, keepdims=True)).astype(bf16)
            dkh = mm(ds, q * sides[h])
            dvh = mm(p.astype(bf16), do * sides[h])
            dk = dkh if dk is None else dk + dkh
            dv = dvh if dv is None else dv + dvh
        place = (j // 4) * width + (j % 4) * 128
        dkv[:, pl.ds(pl.multiple_of(place, 128), 128)] = dk.astype(bf16)
        dkv[:, pl.ds(pl.multiple_of(place + half, 128), 128)] = dv.astype(bf16)

    def chunk(g, yy, side):
        span = pl.ds(pl.multiple_of(((y + yy) % 4) * 256 + side * 128, 128), 128)
        return mm(ctx_t[span, :], dkv[:, g * width : (g + 1) * width])

    def x_rows(d):
        return pl.ds(pl.multiple_of(((x + d) % 4) * 32, 32), 32)

    sent = []
    live = {}

    def begin(g):
        live["core"] = []
        for i in range(4):
            core_out[g, i] = chunk(g, 2 + i, 1 - core).astype(bf16)
            live["core"].append(copy(core_out.at[g, i], core_in.at[g, i], partner))
        for i in range(4):
            acc[g, i] = chunk(g, 2 + i, core)

    def step1(g):
        for c in live["core"]:
            c.wait_recv()
        sent.extend(live["core"])
        acc[g, 0] = acc[g, 0] + core_in[g, 0].astype(f32)
        live["a"], live["b"] = [], []
        for i, d in enumerate((1, 3)):
            a1_out[g, i] = acc[g, 0, :, i * quarter : (i + 1) * quarter].astype(bf16)
            live["a"].append(copy(a1_out.at[g, i], a1_in.at[g, i], y_peer(d)))
        for i in range(1, 4):
            acc[g, i] = acc[g, i] + core_in[g, i].astype(f32)
        for i, d in enumerate((1, 3)):
            cols = slice(half + i * quarter, half + (i + 1) * quarter)
            b1_out[g, i] = acc[g, :, x_rows(2), cols].astype(bf16)
            live["b"].append(copy(b1_out.at[g, i], b1_in.at[g, i], x_peer(d)))

    def step2(g):
        a1, b1 = live["a"], live["b"]
        sent.extend(a1 + b1)
        live["a"], live["b"] = [], []
        for i, d in enumerate((1, 3)):
            lo, hi = slice(i * quarter, (i + 1) * quarter), slice((1 - i) * quarter, (2 - i) * quarter)
            a1[i].wait_recv()
            slot = (3, 1)[i]
            a2_out[g, i, :, lo] = (acc[g, slot, :, lo] + a1_in[g, i].astype(f32)).astype(bf16)
            a2_out[g, i, :, hi] = acc[g, slot, :, hi].astype(bf16)
            live["a"].append(copy(a2_out.at[g, i], a2_in.at[g, i], y_peer(d)))
        for i, d in enumerate((1, 3)):
            lo, hi = slice(i * quarter, (i + 1) * quarter), slice((1 - i) * quarter, (2 - i) * quarter)
            mine = slice(half + i * quarter, half + (i + 1) * quarter)
            rest = slice(half + (1 - i) * quarter, half + (2 - i) * quarter)
            b1[i].wait_recv()
            b2_out[g, i, :, :, lo] = (acc[g, :, x_rows(d), mine] + b1_in[g, i].astype(f32)).astype(bf16)
            b2_out[g, i, :, :, hi] = acc[g, :, x_rows(d), rest].astype(bf16)
            live["b"].append(copy(b2_out.at[g, i], b2_in.at[g, i], x_peer(d)))

    def step3(g):
        a2, b2 = live["a"], live["b"]
        sent.extend(a2 + b2)
        live["a"], live["b"] = [], []
        for c in a2:
            c.wait_recv()
        a_sum[g] = acc[g, 2, :, 0:half] + a2_in[g, 0].astype(f32) + a2_in[g, 1].astype(f32)
        for d in (1, 2, 3):
            a3_out[g, d - 1] = a_sum[g, x_rows(d), :].astype(bf16)
            live["a"].append(copy(a3_out.at[g, d - 1], a3_in.at[g, d - 1], x_peer(d)))
        for c in b2:
            c.wait_recv()
        b_sum[g] = acc[g, :, x_rows(0), half:] + b2_in[g, 0].astype(f32) + b2_in[g, 1].astype(f32)
        for d in (1, 2, 3):
            b3_out[g, d - 1] = b_sum[g, (2 + d) % 4].astype(bf16)
            live["b"].append(copy(b3_out.at[g, d - 1], b3_in.at[g, d - 1], y_peer(d)))

    def step4(g):
        a3, b3 = live["a"], live["b"]
        sent.extend(a3 + b3)
        for c in a3:
            c.wait_recv()
        end = a_sum[g, x_rows(0), :] + (a3_in[g, 0].astype(f32) + a3_in[g, 1].astype(f32) + a3_in[g, 2].astype(f32))
        for i in range(8):
            z_out[g, i, :, 0:half] = end[4 * i : 4 * i + 4]
        for c in b3:
            c.wait_recv()
        end = b_sum[g, 2] + (b3_in[g, 0].astype(f32) + b3_in[g, 1].astype(f32) + b3_in[g, 2].astype(f32))
        for i in range(8):
            z_out[g, i, :, half:] = end[4 * i : 4 * i + 4]
        live["z", g] = [copy(z_out.at[g, (z + d) % 8], z_in.at[g, d - 1], z_peer(d)) for d in range(1, 8)]

    def finish(g):
        sent.extend(live["z", g])
        for c in live["z", g]:
            c.wait_recv()
        grad = z_out[g, z]
        for d in range(1, 8):
            grad = grad + z_in[g, d - 1]
        grad_ref[:, g * half : (g + 1) * half] = grad[:, 0:half]
        grad_ref[:, width + g * half : width + (g + 1) * half] = grad[:, half:]

    def loss_step(before, k, peer_of, ds, slot):
        if not isinstance(before, list):
            before = [before]
        value = l_out[k - 1]
        for i, c in enumerate(before):
            c.wait_recv()
            value = value + l_in[slot + i]
        sent.extend(before)
        l_out[k] = value
        after = slot + len(before)
        return [copy(l_out.at[k], l_in.at[after + i], peer_of(d)) for i, d in enumerate(ds)], after

    @pl.loop(0, 4)
    def _(j):
        backward(j)

    loss_y, slot = loss_step(loss_core, 1, y_peer, (1, 2, 3), 0)
    begin(0)
    backward(4)
    step1(0)
    loss_x, slot = loss_step(loss_y, 2, x_peer, (1, 2, 3), slot)
    backward(5)
    step2(0)
    loss_z, slot = loss_step(loss_x, 3, z_peer, range(1, 8), slot)
    backward(6)
    step3(0)
    backward(7)
    step4(0)
    begin(1)
    total = l_out[3]
    for i, c in enumerate(loss_z):
        c.wait_recv()
        total = total + l_in[slot + i]
    sent.extend(loss_z)
    total_ref[...] = total[0:1, 0:1] / pair_count
    step1(1)
    step2(1)
    finish(0)
    step3(1)
    step4(1)
    finish(1)
    for c in sent:
        c.wait_send()


def reward_and_gradient(mask, label, q, kv, read, ctx, pair_count):
    tokens, width = q.shape
    keys = kv.shape[0]
    f32, bf16 = jnp.float32, jnp.bfloat16
    half, quarter = width // 2, width // 4

    def both(*shape):
        return [pltpu.VMEM((2, *shape), bf16), pltpu.VMEM((2, *shape), bf16)]

    return pl.pallas_call(
        functools.partial(reward_kernel, pair_count),
        out_shape=(
            jax.ShapeDtypeStruct((1, 1), f32),
            jax.ShapeDtypeStruct((1, 1), f32),
            jax.ShapeDtypeStruct((4, 2 * width), f32),
        ),
        in_specs=[SMEM, SMEM] + [VMEM] * 4,
        out_specs=(VMEM, VMEM, VMEM),
        scratch_shapes=[
            pltpu.VMEM((width, keys), bf16),
            pltpu.VMEM((HEADS, keys, tokens), f32),
            pltpu.VMEM((HEADS, 8, tokens), f32),
            pltpu.VMEM((width, tokens), bf16),
            pltpu.VMEM((tokens, width), bf16),
            pltpu.VMEM((width, keys), bf16),
            pltpu.VMEM((keys, 2 * width), bf16),
            pltpu.VMEM((2, 4, 128, width), f32),
            *both(4, 128, width),
            *both(2, 128, quarter),
            *both(2, 4, 32, quarter),
            *both(2, 128, half),
            *both(2, 4, 32, half),
            pltpu.VMEM((2, 128, half), f32),
            pltpu.VMEM((2, 4, 32, half), f32),
            *both(3, 32, half),
            *both(3, 32, half),
            pltpu.VMEM((2, 8, 4, width), f32),
            pltpu.VMEM((2, 7, 4, width), f32),
            pltpu.VMEM((4, 8, 128), f32),
            pltpu.VMEM((14, 8, 128), f32),
            pltpu.SemaphoreType.DMA((64,)),
            pltpu.SemaphoreType.DMA((64,)),
        ],
        compiler_params=pltpu.CompilerParams(
            collective_id=1, has_side_effects=True, vmem_limit_bytes=62 * 2**20
        ),
        name="reward_and_gradient",
    )(mask, label, q, kv, read, ctx)


def local(
    video_stream,
    video_qkv,
    out_weight,
    text_states,
    query_weight,
    kv_weight,
    read_weight,
    block_mask,
    pair_labels,
):
    width = out_weight.shape[1]
    rows = video_stream.shape[2]
    qkv = video_qkv.reshape(rows // 16, 16, 3 * width)
    queries, context, keys_values = prepare(
        qkv, query_weight, out_weight, kv_weight, text_states[0], video_stream.reshape(rows, width)
    )
    pair_count = lax.axis_size("grp") * lax.axis_size("seq")
    reward, loss, kv_grad = reward_and_gradient(
        block_mask[0, 0], pair_labels[0], queries, keys_values, read_weight.reshape(-1, 128), context, pair_count
    )
    return (reward, loss[0, 0], kv_grad)


def solution(mesh):
    placed = (
        P("grp", "seq", None, None),
        P("grp", "seq", None, None),
        P(("grp", "seq"), None),
        P("grp", "seq", None),
        P(("grp", "seq"), None),
        P(("grp", "seq"), None),
        P(),
        P("grp", "seq", None),
        P("grp", "seq"),
    )
    return jax.shard_map(
        local,
        mesh=mesh,
        in_specs=placed,
        out_specs=(P("grp", "seq"), P(), P(("grp", "seq"), None)),
        check_vma=False,
    )
```

time: 188 us -> 178 us (0.947)
  local copies, waits for them, and re-layouts: 10.7 us -> 1.38 us
  Pallas kernels: 174 us -> 172 us
    concatenate x1 -> x0, local copies, waits for them, and re-layouts: 2.54 us -> none  [local(): jnp.concatenate([jnp.pad(query_weight, ((0, 2), (0, 0))), out_weight, kv_...]
    slice x3 -> x0, local copies, waits for them, and re-layouts: 2.43 us -> none  [the longest x2 1.71 us: local(): return (reward[0:1, 0:1], total[0, 0] / pair_count, kv_grad)]
    pallas_call x2 -> x1, Pallas kernels: 69 us -> 67.1 us  [reward_and_gradient(): pl.pallas_call(functools.partial(reward_kernel, pair_count), out_shape=(j...]
where the time goes in v1:
time: 178 us
  Pallas kernels  172 us (97%)
  between operations  4.82 us (3%)
    pallas_call x1, Pallas kernels, prepare(): pl.pallas_call(prepare_kernel, out_shape=(jax.ShapeDtypeStruct((tokens, w...  105 us
    pallas_call x1, Pallas kernels, reward_and_gradient(): pl.pallas_call(functools.partial(reward_kernel, pair_count), out_shape=(j...  67.1 us

profile of v1, /device:TPU:2, one launch (start us, length us, event | category | flops | bytes accessed | tf_op | source)
XLA Modules:
  0.0 178.2 jit_solution(1970043305725387999)
XLA Ops:
  1.3 104.9 %prepare.1 = (bf16[512,1024]{1,0:T(8,128)(2,1)}, bf16[768,1024]{1,0:T(8,128)(2,1)}, bf16[768,2048]{1,0:T(8,128)(2,1)}) custom-call(bf16[16,16,3072]{2,1,0:T(8,128)(2,1)} %bitcast.9, bf16[14,1024]{1,0:T(8,128)(2,1)} %wq_ref.1, bf16[4,1024]{1,0:T(4,128)(2,1)} %wo_ref.1, bf16[4,2048]{1,0:T(4,128)(2,1)} %wkv_ref.1, bf16[512,3584]{1,0:T(8,128)(2,1)} %bitcast.8, ...), custom_call_target="tpu_custom_call" | custom-call | tf_op jit(solution)/shard_map/prepare/pallas_call | solution.py:301
  106.2 67.1 %reward_and_gradient.1 = (f32[1,1]{1,0:T(1,128)}, f32[1,1]{1,0:T(1,128)}, f32[4,2048]{1,0:T(4,128)}) custom-call(s32[3]{0:T(128)} %bitcast.12, s32[1]{0:T(128)} %bitcast.7.label_ref, bf16[512,1024]{1,0:T(8,128)(2,1)} %get-tuple-element.9.q_ref, bf16[768,2048]{1,0:T(8,128)(2,1)} %get-tuple-element.10.kv, f32[8,128]{1,0:T(8,128)} %bitcast.11, ...), custom_call_target="tpu_custom_call" | custom-call | tf_op jit(solution)/shard_map/reward_and_gradient/pallas_call | solution.py:617
  174.6 1.4 copy.18

commit v2 on v1

v2 whole, which is shorter than its diff:
```python
import functools
import itertools
import jax
import jax.numpy as jnp
from jax import lax
from jax.experimental import pallas as pl
from jax.experimental.pallas import tpu as pltpu
from jax.sharding import PartitionSpec as P

HEADS = 16
MESH = pl.DeviceIdType.MESH
EPSILON = 1e-06
NN = (((1,), (0,)), ((), ()))
NT = (((1,), (1,)), ((), ()))
VMEM = pl.BlockSpec(memory_space=pltpu.VMEM)
SMEM = pl.BlockSpec(memory_space=pltpu.SMEM)


def mm(a, b, dims=NN):
    return lax.dot_general(a, b, dims, preferred_element_type=jnp.float32)


def prepare_kernel(
    qkv_ref, wq_ref, wo_ref, wkv_ref, text_ref, stream_ref, q_ref, ctx_ref, kv_ref,
    shard, stage, got, mixed_out, frame, back, text, stream, shards, q_tmp, o_tmp, s_tmp, wq, wo, wkv, halo,
    local_sem, z_send, z_recv, go_send, go_recv, ret_send, ret_recv, w_send, w_recv, h_send, h_recv,
):
    f32, bf16 = jnp.float32, jnp.bfloat16
    grp, seq = lax.axis_index("grp"), lax.axis_index("seq")
    y, core = grp // 2, grp % 2
    x, z = seq // 8, seq % 8
    width = wq.shape[1]
    rows = frame.shape[0]
    quarter = width // 4

    def seq_at(d):
        return ((x + d // 8) % 4) * 8 + (z + d % 8) % 8

    def y_peer(d):
        return (((y + d) % 4) * 2 + core, seq)

    def x_peer(d):
        return (grp, ((x + d) % 4) * 8 + z)

    partner = (y * 2 + 1 - core, seq)
    barrier = pltpu.get_barrier_semaphore()

    locals_ = []
    for part in range(3):
        for side in range(4):
            start = part * width + side * quarter
            locals_.append(pltpu.make_async_copy(
                qkv_ref.at[:, :, start : start + quarter], stage.at[:, side // 2, side % 2, part],
                local_sem.at[part * 4 + side],
            ))
    load_text = pltpu.make_async_copy(text_ref, text, local_sem.at[12])
    load_stream = pltpu.make_async_copy(stream_ref, stream, local_sem.at[13])
    for c in locals_ + [load_text, load_stream]:
        c.start()

    @pl.loop(1, 32)
    def _(d):
        pl.semaphore_signal(barrier, inc=1, device_id=(grp, seq_at(d)), device_id_type=MESH)

    for peer in (partner, y_peer(1), y_peer(3)):
        pl.semaphore_signal(barrier, inc=1, device_id=peer, device_id_type=MESH)
    q_tmp[0:14, :] = wq_ref[...].astype(f32)
    q_tmp[16:20, :] = wo_ref[...].astype(f32)
    q_tmp[20:24, :] = wkv_ref[:, 0:width].astype(f32)
    q_tmp[24:28, :] = wkv_ref[:, width:].astype(f32)
    own = q_tmp[0:32, :].astype(bf16)
    shard[...] = own
    shards[z] = own
    pl.semaphore_wait(barrier, 34)

    def remote(src, dst, sems, i, peer):
        return pltpu.make_async_remote_copy(
            src_ref=src, dst_ref=dst, send_sem=sems[0].at[i], recv_sem=sems[1].at[i],
            device_id=peer, device_id_type=MESH,
        )

    def z_copy(d, k):
        span = pl.ds(16 * k, 16)
        return remote(
            shard.at[span, :], shards.at[z, span, :], (z_send, z_recv), 8 * k + d, (grp, x * 8 + (z + d) % 8)
        )

    def go(d, part):
        t = seq_at(d)
        return remote(
            stage.at[t // 2, t % 2, part], got.at[part, seq], (go_send, go_recv), part * 32 + d, (grp, t)
        )

    def home(part):
        first = seq % 2 * (width // 2) + part * quarter
        return (pl.ds(pl.multiple_of(seq // 2 * 16, 16), 16), pl.ds(pl.multiple_of(first, 128), quarter))

    def ret(d, part):
        t = seq_at(d)
        return remote(
            back.at[part, t], frame.at[home(part)], (ret_send, ret_recv), part * 32 + d, (grp, t)
        )

    for k in (1, 0):
        for d in (4, 3, 5, 2, 6, 1, 7):
            z_copy(d, k).start()
    for c in locals_:
        c.wait()

    for part in range(2):

        @pl.loop(1, 32)
        def _(d, part=part):
            go(d, part).start()

        got[part, seq] = stage[seq // 2, seq % 2, part]

    counter = [0]

    def block(unit, yy, xx, lo, n):
        first = (((y + yy) % 4) * 8 + core * 4 + (x + xx) % 4) * unit + lo
        return pl.ds(pl.multiple_of(first, 16), n)

    def spread(ref, unit, cut, first, second, flip):
        at = (lambda a, b, lo, n: block(unit, b, a, lo, n)) if flip else (lambda a, b, lo, n: block(unit, a, b, lo, n))

        def send(a, b, lo, n, peer):
            i = counter[0]
            counter[0] += 1
            span = at(a, b, lo, n)
            c = remote(ref.at[span, :], ref.at[span, :], (w_send, w_recv), i, peer)
            c.start()
            return c

        started = []

        def out(peer_of, a, b):
            pair = [send(a, b, 0, unit, peer_of(1)), send(a, b, 0, unit, peer_of(3))]
            started.extend(pair)
            return pair

        def on(peer_of, a, b, along_first):
            if along_first:
                pair = [send(a - 1, b, 0, cut, peer_of(1)), send(a + 1, b, cut, unit - cut, peer_of(3))]
            else:
                pair = [send(a, b - 1, 0, cut, peer_of(1)), send(a, b + 1, cut, unit - cut, peer_of(3))]
            started.extend(pair)
            return pair

        def arrived(pair):
            for c in pair:
                c.wait_recv()

        state = {}

        def step0():
            state["f"] = out(first, 0, 0)
            state[0] = out(second, 0, 0)

        def step1():
            arrived(state["f"])
            state["ff"] = on(first, 0, 0, True)
            state[3] = out(second, 3, 0)
            state[1] = out(second, 1, 0)

        def step2():
            arrived(state["ff"])
            state[2] = out(second, 2, 0)

        def forward(a):
            arrived(state[a])
            state["s", a] = on(second, a, 0, False)

        def finish():
            for a in range(4):
                arrived(state["s", a])

        return started, step0, step1, step2, forward, finish

    o_sent, o0, o1, o2, o_on, o_end = spread(wo, 32, 16, x_peer, y_peer, True)
    s_sent, s0, s1, s2, s_on, s_end = spread(wkv, 32, 16, y_peer, x_peer, False)
    q_sent, q0, q1, q2, q_on, q_end = spread(wq, 112, 64, x_peer, y_peer, True)

    for d in range(1, 8):
        z_copy(d, 1).wait()
    for i in range(8):
        w = shards[i, 16:32, :].astype(f32)
        o_tmp[4 * i : 4 * i + 4, :] = w[0:4]
        for k in range(2):
            s_tmp[4 * i : 4 * i + 4, k * width : (k + 1) * width] = w[4 + 4 * k : 8 + 4 * k]
    wo[block(32, 0, 0, 0, 32), :] = o_tmp[...].astype(bf16)
    o0()
    wkv[block(32, 0, 0, 0, 32), :] = s_tmp[...].astype(bf16)
    s0()
    for d in range(1, 8):
        z_copy(d, 0).wait()
    for i in range(8):
        q_tmp[14 * i : 14 * i + 14, :] = shards[i, 0:16, :].astype(f32)[0:14]
    wq[block(112, 0, 0, 0, 112), :] = q_tmp[...].astype(bf16)
    q0()
    o1()
    s1()
    q1()
    o2()
    s2()
    q2()
    for a in (0, 3, 1):
        o_on(a)
        q_on(a)
        s_on(a)

    count = 32 * 16
    lane = lax.broadcasted_iota(jnp.int32, (1, 128), 1)
    sides = [((lane // 64) == h).astype(bf16) for h in range(2)]

    def temporal(part, j):
        cols = slice(j * 128, j * 128 + 128)
        q = got[part, :, 0, :, cols].reshape(count, 128)
        k = got[part, :, 1, :, cols].reshape(count, 128)
        v = got[part, :, 2, :, cols].reshape(count, 128)
        other = (
            lax.broadcasted_iota(jnp.int32, (count, count), 0) % 16
            != lax.broadcasted_iota(jnp.int32, (count, count), 1) % 16
        )
        total = None
        for h in range(2):
            s = mm(q * (sides[h] * jnp.asarray(0.125, bf16)), k, NT)
            s = jnp.where(other, -jnp.inf, s)
            e = jnp.exp(s - jnp.max(s, axis=1, keepdims=True))
            p = (e * (1.0 / jnp.sum(e, axis=1, keepdims=True))).astype(bf16)
            o = mm(p, v * sides[h])
            total = o if total is None else total + o
        back[part, :, :, cols] = total.astype(bf16).reshape(32, 16, 128)

    for part in range(2):

        @pl.loop(1, 32)
        def _(d, part=part):
            go(d, part).wait_recv()

        for j in range(2):
            temporal(part, j)

        @pl.loop(1, 32)
        def _(d, part=part):
            ret(d, part).start()

        frame[home(part)] = back[part, seq]

        if part == 0:
            o_on(2)
            s_on(2)
            q_on(2)

    def to_partner(ref, unit, yy):
        i = counter[0]
        counter[0] += 1
        span = pl.ds(pl.multiple_of((((y + yy) % 4) * 2 + core) * 4 * unit, 16), 4 * unit)
        c = remote(ref.at[span, :], ref.at[span, :], (w_send, w_recv), i, partner)
        c.start()
        return c

    o_core = [to_partner(wo, 32, yy) for yy in (0, 3, 1)]
    q_core = [to_partner(wq, 112, yy) for yy in (0, 3, 1)]
    o_end()
    o_core.append(to_partner(wo, 32, 2))
    s_end()
    s_core = [to_partner(wkv, 32, yy) for yy in (0, 3, 1, 2)]

    for part in range(2):

        @pl.loop(1, 32)
        def _(d, part=part):
            ret(d, part).wait_recv()

    for c in o_core:
        c.wait_recv()
    load_stream.wait()

    halos = []
    part = 64
    for i in range(rows // part):
        span = slice(i * part, (i + 1) * part)
        mixed = (stream[span, :].astype(f32) + mm(frame[span, :], wo[...])).astype(bf16)
        mixed_out[span, :] = mixed
        for s, d in ((0, 1), (1, 31)):
            c = remote(
                mixed_out.at[span, :], halo.at[s, span, :], (h_send, h_recv), 2 * i + s,
                (grp, (seq + d) % 32),
            )
            c.start()
            halos.append(c)

    def keys_values(b, m):
        for c in range(4):
            cols = slice(c * (width // 2), (c + 1) * (width // 2))
            kv_ref[b * rows : (b + 1) * rows, cols] = mm(m, wkv[:, cols]).astype(bf16)

    q_end()
    q_core.append(to_partner(wq, 112, 2))
    for c in s_core:
        c.wait_recv()
    ctx_ref[rows : 2 * rows, :] = mixed_out[...]
    keys_values(1, mixed_out[...])
    for c in q_core:
        c.wait_recv()
    load_text.wait()
    tokens = text.shape[0]
    for i in range(2):
        span = slice(i * (tokens // 2), (i + 1) * (tokens // 2))
        for k in range(2):
            cols = slice(k * (width // 2), (k + 1) * (width // 2))
            q_ref[span, cols] = (mm(text[span, :], wq[:, cols]).astype(bf16) * jnp.asarray(0.125, bf16))
    for c in halos:
        c.wait_recv()
    for s, b in ((0, 0), (1, 2)):
        ctx_ref[b * rows : (b + 1) * rows, :] = halo[s]
        keys_values(b, halo[s])

    for c in halos + o_sent + q_sent + s_sent + o_core + q_core + s_core:
        c.wait_send()

    @pl.loop(1, 32)
    def _(d):
        for part in range(2):
            go(d, part).wait_send()
            ret(d, part).wait_send()


def prepare(qkv, wq, wo, wkv, text, stream):
    f32, bf16 = jnp.float32, jnp.bfloat16
    tokens, depth = text.shape
    rows, width = stream.shape
    any_ = pl.BlockSpec(memory_space=pl.ANY)
    dma = pltpu.SemaphoreType.DMA
    return pl.pallas_call(
        prepare_kernel,
        out_shape=(
            jax.ShapeDtypeStruct((tokens, width), bf16),
            jax.ShapeDtypeStruct((3 * rows, width), bf16),
            jax.ShapeDtypeStruct((3 * rows, 2 * width), bf16),
        ),
        in_specs=[any_, VMEM, VMEM, VMEM, any_, any_],
        out_specs=(VMEM, VMEM, VMEM),
        scratch_shapes=[
            pltpu.VMEM((32, width), bf16),
            pltpu.VMEM((16, 2, 2, 3, 16, width // 4), bf16),
            pltpu.VMEM((2, 32, 3, 16, width // 4), bf16),
            pltpu.VMEM((rows, width), bf16),
            pltpu.VMEM((rows, width), bf16),
            pltpu.VMEM((2, 32, 16, width // 4), bf16),
            pltpu.VMEM((tokens, depth), bf16),
            pltpu.VMEM((rows, width), bf16),
            pltpu.VMEM((8, 32, width), bf16),
            pltpu.VMEM((112, width), f32),
            pltpu.VMEM((32, width), f32),
            pltpu.VMEM((32, 2 * width), f32),
            pltpu.VMEM((depth, width), bf16),
            pltpu.VMEM((width, width), bf16),
            pltpu.VMEM((width, 2 * width), bf16),
            pltpu.VMEM((2, rows, width), bf16),
            dma((16,)), dma((16,)), dma((16,)), dma((64,)), dma((64,)), dma((64,)), dma((64,)),
            dma((96,)), dma((96,)), dma((8,)), dma((8,)),
        ],
        compiler_params=pltpu.CompilerParams(
            collective_id=2, has_side_effects=True, vmem_limit_bytes=56 * 2**20
        ),
        name="prepare",
    )(qkv, wq, wo, wkv, text, stream)


PARTS = (4, 3, 1)


def reward_kernel(
    pair_count, mask_ref, label_ref, q_ref, kv, read_ref, ctx_ref, reward_ref, total_ref, grad_ref,
    vt, exps, inverse, d_out_t, d_out, ctx_t, dkv,
    acc, core_out, core_in, a1_out, a1_in, b1_out, b1_in, a_sum, b_sum, a2_out, a2_in, b2_out, b2_in, z_out, z_in, l_out, l_in, send, recv,
):
    f32, bf16 = jnp.float32, jnp.bfloat16
    tokens, width = q_ref.shape
    rows = kv.shape[0] // 3
    pairs = width // 128
    blocks = [pl.ds(b * rows, rows) for b in range(3)]
    grp, seq = lax.axis_index("grp"), lax.axis_index("seq")
    y, core = grp // 2, grp % 2
    x, z = seq // 8, seq % 8
    parts = list(zip((0, *itertools.accumulate(PARTS)), PARTS))

    def y_peer(d):
        return (((y + d) % 4) * 2 + core, seq)

    def x_peer(d):
        return (grp, ((x + d) % 4) * 8 + z)

    def z_peer(d):
        return (grp, x * 8 + (z + d) % 8)

    partner = (y * 2 + 1 - core, seq)
    peers = [partner] + [y_peer(d) for d in (1, 2, 3)] + [x_peer(d) for d in (1, 2, 3)]
    peers += [z_peer(d) for d in range(1, 8)]
    barrier = pltpu.get_barrier_semaphore()
    for peer in peers:
        pl.semaphore_signal(barrier, inc=1, device_id=peer, device_id_type=MESH)

    count = [0]

    def copy(src, dst, peer):
        i = count[0]
        count[0] += 1
        c = pltpu.make_async_remote_copy(
            src_ref=src, dst_ref=dst, send_sem=send.at[i], recv_sem=recv.at[i],
            device_id=peer, device_id_type=MESH,
        )
        c.start()
        return c

    lane = lax.broadcasted_iota(jnp.int32, (1, 128), 1)
    sides = [((lane // 64) == h).astype(bf16) for h in range(2)]
    bias = [jnp.where(mask_ref[b] == 1, 0.0, -jnp.inf).astype(f32) for b in range(3)]

    def forward(j, squares):
        cols = pl.ds(pl.multiple_of(j * 128, 128), 128)
        vcols = pl.ds(pl.multiple_of(width + j * 128, 128), 128)
        vt[cols, :] = kv[:, vcols].T
        ctx_t[cols, :] = ctx_ref[:, cols].T
        k = kv[:, cols]
        q = q_ref[:, cols]
        for h in range(2):
            s = mm(k, q * sides[h], NT)
            s = [s[b * rows : (b + 1) * rows] for b in range(3)]
            top = [jnp.max(s[b], axis=0, keepdims=True) + bias[b] for b in range(3)]
            top = jnp.maximum(jnp.maximum(top[0], top[1]), top[2])
            total = jnp.zeros((1, tokens), f32)
            for b in range(3):
                e = jnp.exp(s[b] - (top - bias[b]))
                exps[2 * j + h, blocks[b], :] = e
                total = total + jnp.sum(e, axis=0, keepdims=True)
            inv = 1.0 / total
            inverse[2 * j + h] = jnp.broadcast_to(inv, (8, tokens))
            p = (exps[2 * j + h] * inv).astype(bf16)
            mine = pl.ds(pl.multiple_of(j * 128 + h * 64, 64), 64)
            o = mm(vt[mine, :], p)
            acc[j % 4, h * 64 : h * 64 + 64, pl.ds(pl.multiple_of((2 + j // 4) * tokens, 128), tokens)] = o
            squares = squares + jnp.sum(o * o, axis=0, keepdims=True)
        return squares

    squares = lax.fori_loop(0, pairs, forward, jnp.zeros((1, tokens), f32))
    inv_root = 1.0 / jnp.sqrt(squares / width + EPSILON)

    reward = jnp.zeros((1, tokens), f32)
    inner = jnp.zeros((1, tokens), f32)
    for j in range(pairs):
        normed = acc[j % 4, :, (2 + j // 4) * tokens : (3 + j // 4) * tokens] * inv_root
        gates = jax.nn.sigmoid(normed)
        read = jnp.broadcast_to(read_ref[j : j + 1, :], (128, 128)).T[:, 0:1]
        scaled = read * gates
        slope = scaled * (1.0 + normed * (1.0 - gates))
        acc[j % 4, :, (j // 4) * tokens : (j // 4 + 1) * tokens] = slope
        reward = reward + jnp.sum(scaled * normed, axis=0, keepdims=True)
        inner = inner + jnp.sum(slope * normed, axis=0, keepdims=True)

    reward = jnp.sum(reward, axis=1, keepdims=True) / tokens
    signed = 2.0 * label_ref[0].astype(f32) - 1.0
    margin = -signed * reward
    loss = jnp.maximum(margin, 0.0) + jnp.log1p(jnp.exp(-jnp.abs(margin)))
    reward_ref[...] = reward
    l_out[0] = jnp.broadcast_to(loss, (8, 128))
    pl.semaphore_wait(barrier, len(peers))
    loss_core = copy(l_out.at[0], l_in.at[0], partner)
    factor = -signed * jax.nn.sigmoid(margin) / pair_count / tokens
    inner = inner / width

    for j in range(pairs):
        cols = slice(j * 128, (j + 1) * 128)
        normed = acc[j % 4, :, (2 + j // 4) * tokens : (3 + j // 4) * tokens] * inv_root
        d = ((acc[j % 4, :, (j // 4) * tokens : (j // 4 + 1) * tokens] - normed * inner) * (inv_root * factor)).astype(bf16)
        d_out_t[cols, :] = d
        d_out[:, cols] = d.T

    def backward(j):
        cols = slice(j * 128, (j + 1) * 128)
        vcols = slice(width + j * 128, width + (j + 1) * 128)
        v = kv[:, vcols]
        q = q_ref[:, cols]
        do = d_out[:, cols]
        empty = jnp.zeros((64, tokens), bf16)
        dk = dv = None
        for h in range(2):
            mine = d_out_t[j * 128 + h * 64 : j * 128 + h * 64 + 64, :]
            mine = jnp.concatenate([mine, empty] if h == 0 else [empty, mine], axis=0)
            dp = mm(v, mine)
            p = exps[2 * j + h] * inverse[2 * j + h, 0:1, :]
            both = p * dp
            ds = (both - p * jnp.sum(both, axis=0, keepdims=True)).astype(bf16)
            dkh = mm(ds, q * sides[h])
            dvh = mm(p.astype(bf16), do * sides[h])
            dk = dkh if dk is None else dk + dkh
            dv = dvh if dv is None else dv + dvh
        first, size = [p for p in parts if p[0] <= j][-1]
        place, half = first * 128 + j * 128, size * 128
        dkv[:, place : place + 128] = dk.astype(bf16)
        dkv[:, place + half : place + half + 128] = dv.astype(bf16)

    def columns(g):
        first, size = parts[g]
        lo, mid, hi = first * 256, first * 256 + size * 128, (first + size) * 256
        return slice(lo, hi), slice(lo, mid), slice(mid, hi), slice(first * 128, (first + size) * 128)

    def chunk(g, yy, side):
        span = pl.ds(pl.multiple_of(((y + yy) % 4) * 256 + side * 128, 128), 128)
        return mm(ctx_t[span, :], dkv[:, columns(g)[0]])

    def x_rows(d):
        return pl.ds(pl.multiple_of(((x + d) % 4) * 32, 32), 32)

    sent = []
    live = {}

    def arrived(name, g):
        sent.extend(live[name, g])
        for c in live[name, g]:
            c.wait_recv()

    def begin(g):
        both = columns(g)[0]
        live["core", g] = []
        for i in range(4):
            core_out[i, :, both] = chunk(g, 2 + i, 1 - core).astype(bf16)
            live["core", g].append(copy(core_out.at[i, :, both], core_in.at[i, :, both], partner))
        for i in range(4):
            acc[i, :, both] = chunk(g, 2 + i, core)

    def step1(g):
        both, a, b, cols = columns(g)
        arrived("core", g)
        for i in range(4):
            acc[i, :, both] = acc[i, :, both] + core_in[i, :, both].astype(f32)
        live["a1", g], live["b1", g] = [], []
        for d in (2, 1, 3):
            a1_out[d - 1, :, cols] = acc[(d + 2) % 4, :, a].astype(bf16)
            live["a1", g].append(copy(a1_out.at[d - 1, :, cols], a1_in.at[d - 1, :, cols], y_peer(d)))
            b1_out[d - 1, :, :, cols] = acc[:, x_rows(d), b].astype(bf16)
            live["b1", g].append(copy(b1_out.at[d - 1, :, :, cols], b1_in.at[d - 1, :, :, cols], x_peer(d)))

    def total_of(ref, cols):
        parts_ = [ref[(d, *[slice(None)] * (len(ref.shape) - 2), cols)].astype(f32) for d in range(3)]
        return parts_[0] + parts_[1] + parts_[2]

    def step2(g):
        both, a, b, cols = columns(g)
        live["a2", g], live["b2", g] = [], []
        arrived("a1", g)
        a_sum[:, cols] = acc[2, :, a] + total_of(a1_in, cols)
        for d in (2, 1, 3):
            a2_out[d - 1, :, cols] = a_sum[x_rows(d), cols].astype(bf16)
            live["a2", g].append(copy(a2_out.at[d - 1, :, cols], a2_in.at[d - 1, :, cols], x_peer(d)))
        arrived("b1", g)
        b_sum[:, :, cols] = acc[:, x_rows(0), b] + total_of(b1_in, cols)
        for d in (2, 1, 3):
            b2_out[d - 1, :, cols] = b_sum[(2 + d) % 4, :, cols].astype(bf16)
            live["b2", g].append(copy(b2_out.at[d - 1, :, cols], b2_in.at[d - 1, :, cols], y_peer(d)))

    def step3(g):
        both, a, b, cols = columns(g)
        arrived("a2", g)
        end = a_sum[x_rows(0), cols] + total_of(a2_in, cols)
        for i in range(8):
            z_out[i, :, a] = end[4 * i : 4 * i + 4]
        arrived("b2", g)
        end = b_sum[2, :, cols] + total_of(b2_in, cols)
        for i in range(8):
            z_out[i, :, b] = end[4 * i : 4 * i + 4]
        live["z", g] = [
            copy(z_out.at[(z + d) % 8, :, both], z_in.at[d - 1, :, both], z_peer(d)) for d in (4, 3, 5, 2, 6, 1, 7)
        ]

    def finish(g):
        both, a, b, cols = columns(g)
        arrived("z", g)
        grad = z_out[z, :, both]
        for d in range(1, 8):
            grad = grad + z_in[d - 1, :, both]
        size = parts[g][1] * 128
        grad_ref[:, cols] = grad[:, 0:size]
        grad_ref[:, width + cols.start : width + cols.stop] = grad[:, size:]

    def loss_step(before, k, peer_of, ds, slot):
        if not isinstance(before, list):
            before = [before]
        value = l_out[k - 1]
        for i, c in enumerate(before):
            c.wait_recv()
            value = value + l_in[slot + i]
        sent.extend(before)
        l_out[k] = value
        after = slot + len(before)
        return [copy(l_out.at[k], l_in.at[after + i], peer_of(d)) for i, d in enumerate(ds)], after

    for j in range(0, 4):
        backward(j)
    loss_y, slot = loss_step(loss_core, 1, y_peer, (1, 2, 3), 0)
    begin(0)
    backward(4)
    step1(0)
    backward(5)
    loss_x, slot = loss_step(loss_y, 2, x_peer, (1, 2, 3), slot)
    backward(6)
    begin(1)
    step2(0)
    step1(1)
    backward(7)
    loss_z, slot = loss_step(loss_x, 3, z_peer, range(1, 8), slot)
    begin(2)
    step3(0)
    step1(2)
    step2(1)
    finish(0)
    step2(2)
    step3(1)
    total = l_out[3]
    for i, c in enumerate(loss_z):
        c.wait_recv()
        total = total + l_in[slot + i]
    sent.extend(loss_z)
    total_ref[...] = total[0:1, 0:1] / pair_count
    step3(2)
    finish(1)
    finish(2)
    for c in sent:
        c.wait_send()


def reward_and_gradient(mask, label, q, kv, read, ctx, pair_count):
    tokens, width = q.shape
    keys = kv.shape[0]
    f32, bf16 = jnp.float32, jnp.bfloat16

    def both(*shape):
        return [pltpu.VMEM(shape, bf16), pltpu.VMEM(shape, bf16)]

    return pl.pallas_call(
        functools.partial(reward_kernel, pair_count),
        out_shape=(
            jax.ShapeDtypeStruct((1, 1), f32),
            jax.ShapeDtypeStruct((1, 1), f32),
            jax.ShapeDtypeStruct((4, 2 * width), f32),
        ),
        in_specs=[SMEM, SMEM] + [VMEM] * 4,
        out_specs=(VMEM, VMEM, VMEM),
        scratch_shapes=[
            pltpu.VMEM((width, keys), bf16),
            pltpu.VMEM((HEADS, keys, tokens), f32),
            pltpu.VMEM((HEADS, 8, tokens), f32),
            pltpu.VMEM((width, tokens), bf16),
            pltpu.VMEM((tokens, width), bf16),
            pltpu.VMEM((width, keys), bf16),
            pltpu.VMEM((keys, 2 * width), bf16),
            pltpu.VMEM((4, 128, 2 * width), f32),
            *both(4, 128, 2 * width),
            *both(3, 128, width),
            *both(3, 4, 32, width),
            pltpu.VMEM((128, width), f32),
            pltpu.VMEM((4, 32, width), f32),
            *both(3, 32, width),
            *both(3, 32, width),
            pltpu.VMEM((8, 4, 2 * width), f32),
            pltpu.VMEM((7, 4, 2 * width), f32),
            pltpu.VMEM((4, 8, 128), f32),
            pltpu.VMEM((14, 8, 128), f32),
            pltpu.SemaphoreType.DMA((128,)),
            pltpu.SemaphoreType.DMA((128,)),
        ],
        compiler_params=pltpu.CompilerParams(
            collective_id=1, has_side_effects=True, vmem_limit_bytes=62 * 2**20
        ),
        name="reward_and_gradient",
    )(mask, label, q, kv, read, ctx)


def local(
    video_stream,
    video_qkv,
    out_weight,
    text_states,
    query_weight,
    kv_weight,
    read_weight,
    block_mask,
    pair_labels,
):
    width = out_weight.shape[1]
    rows = video_stream.shape[2]
    qkv = video_qkv.reshape(rows // 16, 16, 3 * width)
    queries, context, keys_values = prepare(
        qkv, query_weight, out_weight, kv_weight, text_states[0], video_stream.reshape(rows, width)
    )
    pair_count = lax.axis_size("grp") * lax.axis_size("seq")
    reward, loss, kv_grad = reward_and_gradient(
        block_mask[0, 0], pair_labels[0], queries, keys_values, read_weight.reshape(-1, 128), context, pair_count
    )
    return (reward, loss[0, 0], kv_grad)


def solution(mesh):
    placed = (
        P("grp", "seq", None, None),
        P("grp", "seq", None, None),
        P(("grp", "seq"), None),
        P("grp", "seq", None),
        P(("grp", "seq"), None),
        P(("grp", "seq"), None),
        P(),
        P("grp", "seq", None),
        P("grp", "seq"),
    )
    return jax.shard_map(
        local,
        mesh=mesh,
        in_specs=placed,
        out_specs=(P("grp", "seq"), P(), P(("grp", "seq"), None)),
        check_vma=False,
    )
```

time: 178 us -> 161 us (0.904)
  Pallas kernels: 172 us -> 155 us
    pallas_call x1, Pallas kernels: 67.1 us -> 56.7 us  [reward_and_gradient(): pl.pallas_call(functools.partial(reward_kernel, pair_count), out_shape=(j...]
    pallas_call x1, Pallas kernels: 105 us -> 98.3 us  [prepare(): pl.pallas_call(prepare_kernel, out_shape=(jax.ShapeDtypeStruct((tokens, w...]
where the time goes in v2:
time: 161 us
  Pallas kernels  155 us (96%)
  between operations  4.82 us (3%)
    pallas_call x1, Pallas kernels, prepare(): pl.pallas_call(prepare_kernel, out_shape=(jax.ShapeDtypeStruct((tokens, w...  98.3 us
    pallas_call x1, Pallas kernels, reward_and_gradient(): pl.pallas_call(functools.partial(reward_kernel, pair_count), out_shape=(j...  56.7 us

profile of v2, /device:TPU:2, one launch (start us, length us, event | category | flops | bytes accessed | tf_op | source)
XLA Modules:
  0.0 161.2 jit_solution(12298616860560318797)
XLA Ops:
  1.3 98.3 %prepare.1 = (bf16[512,1024]{1,0:T(8,128)(2,1)}, bf16[768,1024]{1,0:T(8,128)(2,1)}, bf16[768,2048]{1,0:T(8,128)(2,1)}) custom-call(bf16[16,16,3072]{2,1,0:T(8,128)(2,1)} %bitcast.9, bf16[14,1024]{1,0:T(8,128)(2,1)} %wq_ref.1, bf16[4,1024]{1,0:T(4,128)(2,1)} %wo_ref.1, bf16[4,2048]{1,0:T(4,128)(2,1)} %wkv_ref.1, bf16[512,3584]{1,0:T(8,128)(2,1)} %bitcast.8, ...), custom_call_target="tpu_custom_call" | custom-call | tf_op jit(solution)/shard_map/prepare/pallas_call | solution.py:336
  99.6 56.7 %reward_and_gradient.1 = (f32[1,1]{1,0:T(1,128)}, f32[1,1]{1,0:T(1,128)}, f32[4,2048]{1,0:T(4,128)}) custom-call(s32[3]{0:T(128)} %bitcast.12, s32[1]{0:T(128)} %bitcast.7.label_ref, bf16[512,1024]{1,0:T(8,128)(2,1)} %get-tuple-element.9.q_ref, bf16[768,2048]{1,0:T(8,128)(2,1)} %get-tuple-element.10.kv, f32[8,128]{1,0:T(8,128)} %bitcast.11, ...), custom_call_target="tpu_custom_call" | custom-call | tf_op jit(solution)/shard_map/reward_and_gradient/pallas_call | solution.py:642
  157.6 1.4 copy.18
